TPU v7x, 32 devices: a whole 2x2x4 slice. The times are simulated.
32 devices in a mesh: frame: 4 (over z), tile: 8 (over y, x, core).
Axes of the slice: x: 2, y: 2, z: 4, core: 2. Of those that a mesh axis runs over, the one named last changes fastest.
Arguments:
- query_tokens: bfloat16 [16, 3072, 1536], P('frame', 'tile'), may hold values from -6 to 6
- key_tokens: bfloat16 [16, 3072, 1536], P('frame', 'tile'), may hold values from -6 to 6
- value_tokens: bfloat16 [16, 3072, 1536], P('frame', 'tile'), may hold values from -6 to 6
- cached_out: bfloat16 [16, 3072, 1536], P('frame', 'tile'), may hold values from -6 to 6
- pattern: int32 [16, 24, 6], P('frame', 'tile'), may hold values from 0 to 1, as said below
- refresh: int32 [16, 24], P('frame', 'tile'), may hold values from 0 to 1, as said below
Outputs:
- refreshed: bfloat16 [16, 3072, 1536], P('frame', 'tile')
Inputs may be any that keep to these rules, and one draw needn't show every extreme that they name: `pattern`: entries 0, 1, 2 (a block's left neighbour, itself and its right neighbour in its own frame) are 1. `refresh`: on the blocks of one device (frames t * 4 to t * 4 + 3, spatial blocks s * 3 to s * 3 + 2), the first and the last spatial block of the device's first frame are flagged, at most 9 blocks are flagged, and some device has exactly 9.
All inputs are finite; a program needn't handle non-finite values.
Results may differ from a plain program's by a relative error of at most 0.004.
Values may be sent and summed in bfloat16 or wider, within the bound.
A program may use at most 128 MiB of HBM per device.

v0:
```python
import jax
import jax.numpy as jnp
from jax import lax
from jax.sharding import PartitionSpec as P

HEADS = 12
HEAD_DIM = 128
BLK = 128
CAP = 9


def extended_2(cells, sides, width):
    for axis, dim in sides:
        count = lax.axis_size(axis)
        ends = count - 1
        head = lax.slice_in_dim(cells, 0, width, axis=dim)
        tail = lax.slice_in_dim(cells, cells.shape[dim] - width, cells.shape[dim], axis=dim)
        cells = jnp.concatenate(
            [
                lax.ppermute(tail, axis, [(i, (i + 1) % count) for i in range(ends)]),
                cells,
                lax.ppermute(head, axis, [((i + 1) % count, i) for i in range(ends)]),
            ],
            axis=dim,
        )
    return cells


def from_behind(block, axis, distance):
    devices = range(lax.axis_size(axis))
    route = [(i - distance, i) for i in devices if i - distance in devices]
    return lax.ppermute(block, axis, route)


def attend_block(query_rows, key_rows, value_rows, allowed):
    queries_h = query_rows.reshape(BLK, HEADS, HEAD_DIM)
    keys_h = key_rows.reshape(6 * BLK, HEADS, HEAD_DIM)
    values_h = value_rows.reshape(6 * BLK, HEADS, HEAD_DIM)
    scores = jnp.einsum(
        "qhe,khe->hqk", queries_h, keys_h, preferred_element_type=jnp.float32
    ) * HEAD_DIM ** (-0.5)
    key_mask = jnp.repeat(allowed > 0, BLK)
    scores = jnp.where(key_mask[None, None, :], scores, -jnp.inf)
    row_max = jnp.max(scores, axis=-1, keepdims=True)
    exponentials = jnp.exp(scores - row_max)
    weights = (exponentials / jnp.sum(exponentials, axis=-1, keepdims=True)).astype(jnp.bfloat16)
    attended = jnp.einsum("hqk,khe->qhe", weights, values_h, preferred_element_type=jnp.float32)
    return attended.reshape(BLK, HEADS * HEAD_DIM).astype(jnp.bfloat16)


def local(query_tokens, key_tokens, value_tokens, cached_out, pattern, refresh):
    frames_here, tokens_here, row_width = query_tokens.shape
    blocks_here = tokens_here // BLK
    joined = jnp.concatenate([key_tokens, value_tokens], axis=2)
    spatial_halo = extended_2(joined, (("tile", 1),), BLK)
    previous = from_behind(spatial_halo[frames_here - 1 :], "frame", 1)
    extended = jnp.concatenate([previous, spatial_halo], axis=0)
    frame_base = lax.axis_index("frame") * frames_here
    block_base = lax.axis_index("tile") * blocks_here
    blocks_all = blocks_here * lax.axis_size("tile")
    neighbour = jnp.arange(6, dtype=jnp.int32)
    offsets = neighbour % 3 - 1
    frame_lags = neighbour // 3
    total_blocks = frames_here * blocks_here
    query_blocks = query_tokens.reshape(total_blocks, BLK, row_width)
    cached_blocks = cached_out.reshape(total_blocks, BLK, row_width)
    flag_list = refresh.reshape(total_blocks)
    pattern_list = pattern.reshape(total_blocks, 6)

    def attend_one(position):
        frame_index = position // blocks_here
        block_index = position % blocks_here
        pieces = []
        for frames_back in (0, 1):
            window = lax.dynamic_slice(
                extended,
                (frame_index + 1 - frames_back, block_index * BLK, 0),
                (1, 3 * BLK, 2 * row_width),
            )
            pieces.append(window[0])
        gathered = jnp.concatenate(pieces, axis=0)
        spatial = block_base + block_index + offsets
        inside = (
            (frame_base + frame_index - frame_lags >= 0) & (spatial >= 0) & (spatial < blocks_all)
        )
        allowed = jnp.where(inside, pattern_list[position], 0)
        return attend_block(
            query_blocks[position], gathered[:, :row_width], gathered[:, row_width:], allowed
        )

    slots_used = jnp.argsort(1 - flag_list, stable=True)[:CAP]
    attended = lax.map(attend_one, slots_used)
    cached_rows = cached_blocks[slots_used]
    updated = jnp.where(flag_list[slots_used][:, None, None] > 0, attended, cached_rows)
    output = cached_blocks.at[slots_used].set(updated)
    return output.reshape(frames_here, tokens_here, row_width)


def solution(mesh):
    placed = (
        P("frame", "tile", None),
        P("frame", "tile", None),
        P("frame", "tile", None),
        P("frame", "tile", None),
        P("frame", "tile", None),
        P("frame", "tile"),
    )
    return jax.shard_map(
        local, mesh=mesh, in_specs=placed, out_specs=P("frame", "tile", None), check_vma=False
    )
```

profile of v0, /device:TPU:20, one launch (start us, length us, event | category | flops | bytes accessed | tf_op | source)
XLA Modules:
  0.0 433.7 jit_solution(3075338617293675116)
XLA Ops:
  0.0 4.8 %copy.41 = bf16[4,384,1536]{2,1,0:T(8,128)(2,1)} copy(bf16[4,384,1536]{2,1,0:T(8,128)(2,1)} %param.11) | data formatting | bytes 9437184
  4.8 6.7 %copy.18 = bf16[4,384,1536]{1,2,0:T(8,128)(2,1)} copy(bf16[4,384,1536]{2,1,0:T(8,128)(2,1)} %param.9) | data formatting | bytes 9437184 | tf_op args[1]
  11.5 6.7 %copy.19 = bf16[4,384,1536]{1,2,0:T(8,128)(2,1)} copy(bf16[4,384,1536]{2,1,0:T(8,128)(2,1)} %param.10) | data formatting | bytes 9437184 | tf_op args[2]
  18.2 3.2 pad_maximum_fusion.5
  21.4 2.2 collective-permute-start
  23.6 4.5 %collective-permute-start.1 = (bf16[4,128,3072]{1,2,0:T(8,128)(2,1)S(1)}, bf16[4,128,3072]{1,2,0:T(8,128)(2,1)S(1)}, u32[]{:S(2)}, u32[]{:S(2)}) collective-permute-start(bf16[4,128,3072]{1,2,0:T(8,128)(2,1)S(1)} %get-tuple-element.294), channel_id=1, source_target_pairs={{1,0},{2,1},{3,2},{4,3},{5,4},{6,5},{7,6},{9,8},{10,9},{11,10},{12... | collective-permute-start | bytes 9437192 | tf_op jit(solution)/shard_map/ppermute | solution.py:22
  28.1 63.9 %collective-permute-done = bf16[4,128,3072]{1,2,0:T(8,128)(2,1)S(1)} collective-permute-done((bf16[4,128,3072]{1,2,0:T(8,128)(2,1)S(1)}, bf16[4,128,3072]{1,2,0:T(8,128)(2,1)S(1)}, u32[]{:S(2)}, u32[]{:S(2)}) %collective-permute-start) | collective-permute-done | bytes 3145760 | tf_op jit(solution)/shard_map/ppermute | solution.py:20
  92.0 0.9 collective-permute-done.1
  92.9 8.0 %pad_maximum_fusion.1 = bf16[1,640,3072]{1,2,0:T(8,128)(2,1)} fusion(bf16[4,128,3072]{1,2,0:T(8,128)(2,1)S(1)} %collective-permute-done.1, bf16[4,128,3072]{1,2,0:T(8,128)(2,1)S(1)} %collective-permute-done, bf16[4,384,1536]{1,2,0:T(8,128)(2,1)S(1)} %copy-done, bf16[4,384,1536]{1,2,0:T(8,128)(2,1)S(1)} %bitcast.50), kind=kLoop, calls=%fused_computation.40 | loop fusion | flops 15728640 | bytes 19660800 | tf_op jit(solution)/shard_map/concatenate | solution.py:18
  101.0 3.7 collective-permute-start.2
  104.8 1.3 sort.17
  106.8 5.1 %gather_fusion.1 = bf16[9,128,1536]{2,1,0:T(8,128)(2,1)} fusion(bf16[12,128,1536]{2,1,0:T(8,128)(2,1)} %bitcast.53, s32[1024]{0:T(1024)S(1)} %pad_clamp_fusion), kind=kCustom, calls=%fused_computation.1 | custom fusion | bytes 7077924 | tf_op jit(solution)/shard_map/gather | solution.py:93
  111.9 74.5 %collective-permute-done.2 = bf16[1,640,3072]{1,2,0:T(8,128)(2,1)} collective-permute-done((bf16[1,640,3072]{1,2,0:T(8,128)(2,1)}, bf16[1,640,3072]{1,2,0:T(8,128)(2,1)}, u32[]{:S(2)}, u32[]{:S(2)}) %collective-permute-start.2) | collective-permute-done | bytes 3932192 | tf_op jit(solution)/shard_map/ppermute | solution.py:32
  186.4 17.0 %maximum_maximum_fusion = bf16[5,640,3072]{1,2,0:T(8,128)(2,1)} fusion(bf16[4,128,3072]{1,2,0:T(8,128)(2,1)} %copy-done.3, bf16[4,384,1536]{1,2,0:T(8,128)(2,1)} %copy.19, bf16[4,384,1536]{1,2,0:T(8,128)(2,1)} %copy.18, bf16[4,128,3072]{1,2,0:T(8,128)(2,1)S(1)} %copy-done.2, bf16[1,640,3072]{1,2,0:T(8,128)(2,1)} %collective-permute-done.2), kind=kLoop, calls=%fused_computation.39 | loop fusion | flops 98304000 | bytes 39321600 | tf_op jit(solution)/shard_map/concatenate | solution.py:57
  203.5 216.1 %while.16 = (s32[]{:T(128)}, bf16[9,128,1536]{2,1,0:T(8,128)(2,1)}, s32[9]{0:T(128)S(1)}, bf16[5,640,3072]{1,2,0:T(8,128)(2,1)}, s32[]{:T(128)}, /*index=5*/s32[...) while((s32[]{:T(128)}, bf16[9,128,1536]{2,1,0:T(8,128)(2,1)}, ...), condition=%wide.region_4.5_spmd.clone, body=%wide.region_1.4_spmd.clone.sunk | while | flops 620692352 | bytes 36977168 | solution.py:92
  206.0 2.9 dynamic-slice_bitcast_fusion.3
  208.9 5.6 %pad_maximum_fusion.7 = (bf16[768,1536]{0,1:T(8,128)(2,1)}, bf16[768,1536]{0,1:T(8,128)(2,1)S(1)}) fusion(bf16[384,3072]{0,1:T(8,128)(2,1)S(1)} %get-tuple-element.352, bf16[384,3072]{0,1:T(8,128)(2,1)S(1)} %get-tuple-element.353), kind=kLoop, calls=%fused_computation.13.clone.1 | loop fusion | flops 9437184 | bytes 9437184 | tf_op jit(solution)/shard_map/while/body/eval_jaxpr/concatenate | solution.py:81
  216.5 1.0 constant_dynamic-slice_fusion.3
  217.8 5.5 %fusion.38 = (f32[12,128]{1,0:T(8,128)S(1)}, f32[12,128,768]{2,1,0:T(8,128)}) fusion(pred[768]{0:T(1024)(128)(4,1)S(1)} %broadcast_bitcast_fusion.2, bf16[128,12,128]{0,2,1:T(8,128)(2,1)S(1)} %bitcast.55, bf16[768,12,128]{0,2,1:T(8,128)(2,1)} %bitcast.52), kind=kOutput, calls=%fused_computation.50.clone.1 | convolution fusion | flops 306709248 | bytes 7478016 | tf_op jit(solution)/shard_map/while/body/eval_jaxpr/sub | solution.py:45
  223.3 3.2 fusion.39
  230.0 2.9 dynamic-slice_bitcast_fusion.3
  232.9 5.6 %pad_maximum_fusion.7 = (bf16[768,1536]{0,1:T(8,128)(2,1)}, bf16[768,1536]{0,1:T(8,128)(2,1)S(1)}) fusion(bf16[384,3072]{0,1:T(8,128)(2,1)S(1)} %get-tuple-element.352, bf16[384,3072]{0,1:T(8,128)(2,1)S(1)} %get-tuple-element.353), kind=kLoop, calls=%fused_computation.13.clone.1 | loop fusion | flops 9437184 | bytes 9437184 | tf_op jit(solution)/shard_map/while/body/eval_jaxpr/concatenate | solution.py:81
  240.5 1.0 constant_dynamic-slice_fusion.3
  241.7 5.5 %fusion.38 = (f32[12,128]{1,0:T(8,128)S(1)}, f32[12,128,768]{2,1,0:T(8,128)}) fusion(pred[768]{0:T(1024)(128)(4,1)S(1)} %broadcast_bitcast_fusion.2, bf16[128,12,128]{0,2,1:T(8,128)(2,1)S(1)} %bitcast.55, bf16[768,12,128]{0,2,1:T(8,128)(2,1)} %bitcast.52), kind=kOutput, calls=%fused_computation.50.clone.1 | convolution fusion | flops 306709248 | bytes 7478016 | tf_op jit(solution)/shard_map/while/body/eval_jaxpr/sub | solution.py:45
  247.3 3.2 fusion.39
  250.7 0.8 constant_dynamic-update-slice_fusion.2
  254.0 2.9 dynamic-slice_bitcast_fusion.3
  256.9 5.6 %pad_maximum_fusion.7 = (bf16[768,1536]{0,1:T(8,128)(2,1)}, bf16[768,1536]{0,1:T(8,128)(2,1)S(1)}) fusion(bf16[384,3072]{0,1:T(8,128)(2,1)S(1)} %get-tuple-element.352, bf16[384,3072]{0,1:T(8,128)(2,1)S(1)} %get-tuple-element.353), kind=kLoop, calls=%fused_computation.13.clone.1 | loop fusion | flops 9437184 | bytes 9437184 | tf_op jit(solution)/shard_map/while/body/eval_jaxpr/concatenate | solution.py:81
  264.5 1.0 constant_dynamic-slice_fusion.3
  265.8 5.5 %fusion.38 = (f32[12,128]{1,0:T(8,128)S(1)}, f32[12,128,768]{2,1,0:T(8,128)}) fusion(pred[768]{0:T(1024)(128)(4,1)S(1)} %broadcast_bitcast_fusion.2, bf16[128,12,128]{0,2,1:T(8,128)(2,1)S(1)} %bitcast.55, bf16[768,12,128]{0,2,1:T(8,128)(2,1)} %bitcast.52), kind=kOutput, calls=%fused_computation.50.clone.1 | convolution fusion | flops 306709248 | bytes 7478016 | tf_op jit(solution)/shard_map/while/body/eval_jaxpr/sub | solution.py:45
  271.3 3.2 fusion.39
  278.1 2.9 dynamic-slice_bitcast_fusion.3
  280.9 5.6 %pad_maximum_fusion.7 = (bf16[768,1536]{0,1:T(8,128)(2,1)}, bf16[768,1536]{0,1:T(8,128)(2,1)S(1)}) fusion(bf16[384,3072]{0,1:T(8,128)(2,1)S(1)} %get-tuple-element.352, bf16[384,3072]{0,1:T(8,128)(2,1)S(1)} %get-tuple-element.353), kind=kLoop, calls=%fused_computation.13.clone.1 | loop fusion | flops 9437184 | bytes 9437184 | tf_op jit(solution)/shard_map/while/body/eval_jaxpr/concatenate | solution.py:81
  288.5 1.0 constant_dynamic-slice_fusion.3
  289.8 5.5 %fusion.38 = (f32[12,128]{1,0:T(8,128)S(1)}, f32[12,128,768]{2,1,0:T(8,128)}) fusion(pred[768]{0:T(1024)(128)(4,1)S(1)} %broadcast_bitcast_fusion.2, bf16[128,12,128]{0,2,1:T(8,128)(2,1)S(1)} %bitcast.55, bf16[768,12,128]{0,2,1:T(8,128)(2,1)} %bitcast.52), kind=kOutput, calls=%fused_computation.50.clone.1 | convolution fusion | flops 306709248 | bytes 7478016 | tf_op jit(solution)/shard_map/while/body/eval_jaxpr/sub | solution.py:45
  295.3 3.2 fusion.39
  302.1 2.9 dynamic-slice_bitcast_fusion.3
  304.9 5.6 %pad_maximum_fusion.7 = (bf16[768,1536]{0,1:T(8,128)(2,1)}, bf16[768,1536]{0,1:T(8,128)(2,1)S(1)}) fusion(bf16[384,3072]{0,1:T(8,128)(2,1)S(1)} %get-tuple-element.352, bf16[384,3072]{0,1:T(8,128)(2,1)S(1)} %get-tuple-element.353), kind=kLoop, calls=%fused_computation.13.clone.1 | loop fusion | flops 9437184 | bytes 9437184 | tf_op jit(solution)/shard_map/while/body/eval_jaxpr/concatenate | solution.py:81
  312.5 1.0 constant_dynamic-slice_fusion.3
  313.8 5.5 %fusion.38 = (f32[12,128]{1,0:T(8,128)S(1)}, f32[12,128,768]{2,1,0:T(8,128)}) fusion(pred[768]{0:T(1024)(128)(4,1)S(1)} %broadcast_bitcast_fusion.2, bf16[128,12,128]{0,2,1:T(8,128)(2,1)S(1)} %bitcast.55, bf16[768,12,128]{0,2,1:T(8,128)(2,1)} %bitcast.52), kind=kOutput, calls=%fused_computation.50.clone.1 | convolution fusion | flops 306709248 | bytes 7478016 | tf_op jit(solution)/shard_map/while/body/eval_jaxpr/sub | solution.py:45
  319.3 3.2 fusion.39
  326.0 2.9 dynamic-slice_bitcast_fusion.3
  328.9 5.6 %pad_maximum_fusion.7 = (bf16[768,1536]{0,1:T(8,128)(2,1)}, bf16[768,1536]{0,1:T(8,128)(2,1)S(1)}) fusion(bf16[384,3072]{0,1:T(8,128)(2,1)S(1)} %get-tuple-element.352, bf16[384,3072]{0,1:T(8,128)(2,1)S(1)} %get-tuple-element.353), kind=kLoop, calls=%fused_computation.13.clone.1 | loop fusion | flops 9437184 | bytes 9437184 | tf_op jit(solution)/shard_map/while/body/eval_jaxpr/concatenate | solution.py:81
  336.5 1.0 constant_dynamic-slice_fusion.3
  337.8 5.5 %fusion.38 = (f32[12,128]{1,0:T(8,128)S(1)}, f32[12,128,768]{2,1,0:T(8,128)}) fusion(pred[768]{0:T(1024)(128)(4,1)S(1)} %broadcast_bitcast_fusion.2, bf16[128,12,128]{0,2,1:T(8,128)(2,1)S(1)} %bitcast.55, bf16[768,12,128]{0,2,1:T(8,128)(2,1)} %bitcast.52), kind=kOutput, calls=%fused_computation.50.clone.1 | convolution fusion | flops 306709248 | bytes 7478016 | tf_op jit(solution)/shard_map/while/body/eval_jaxpr/sub | solution.py:45
  343.3 3.2 fusion.39
  346.7 0.8 constant_dynamic-update-slice_fusion.2
  350.1 2.9 dynamic-slice_bitcast_fusion.3
  353.0 5.6 %pad_maximum_fusion.7 = (bf16[768,1536]{0,1:T(8,128)(2,1)}, bf16[768,1536]{0,1:T(8,128)(2,1)S(1)}) fusion(bf16[384,3072]{0,1:T(8,128)(2,1)S(1)} %get-tuple-element.352, bf16[384,3072]{0,1:T(8,128)(2,1)S(1)} %get-tuple-element.353), kind=kLoop, calls=%fused_computation.13.clone.1 | loop fusion | flops 9437184 | bytes 9437184 | tf_op jit(solution)/shard_map/while/body/eval_jaxpr/concatenate | solution.py:81
  360.6 1.0 constant_dynamic-slice_fusion.3
  361.9 5.5 %fusion.38 = (f32[12,128]{1,0:T(8,128)S(1)}, f32[12,128,768]{2,1,0:T(8,128)}) fusion(pred[768]{0:T(1024)(128)(4,1)S(1)} %broadcast_bitcast_fusion.2, bf16[128,12,128]{0,2,1:T(8,128)(2,1)S(1)} %bitcast.55, bf16[768,12,128]{0,2,1:T(8,128)(2,1)} %bitcast.52), kind=kOutput, calls=%fused_computation.50.clone.1 | convolution fusion | flops 306709248 | bytes 7478016 | tf_op jit(solution)/shard_map/while/body/eval_jaxpr/sub | solution.py:45
  367.4 3.2 fusion.39
  374.1 2.9 dynamic-slice_bitcast_fusion.3
  377.0 5.6 %pad_maximum_fusion.7 = (bf16[768,1536]{0,1:T(8,128)(2,1)}, bf16[768,1536]{0,1:T(8,128)(2,1)S(1)}) fusion(bf16[384,3072]{0,1:T(8,128)(2,1)S(1)} %get-tuple-element.352, bf16[384,3072]{0,1:T(8,128)(2,1)S(1)} %get-tuple-element.353), kind=kLoop, calls=%fused_computation.13.clone.1 | loop fusion | flops 9437184 | bytes 9437184 | tf_op jit(solution)/shard_map/while/body/eval_jaxpr/concatenate | solution.py:81
  384.6 1.0 constant_dynamic-slice_fusion.3
  385.8 5.5 %fusion.38 = (f32[12,128]{1,0:T(8,128)S(1)}, f32[12,128,768]{2,1,0:T(8,128)}) fusion(pred[768]{0:T(1024)(128)(4,1)S(1)} %broadcast_bitcast_fusion.2, bf16[128,12,128]{0,2,1:T(8,128)(2,1)S(1)} %bitcast.55, bf16[768,12,128]{0,2,1:T(8,128)(2,1)} %bitcast.52), kind=kOutput, calls=%fused_computation.50.clone.1 | convolution fusion | flops 306709248 | bytes 7478016 | tf_op jit(solution)/shard_map/while/body/eval_jaxpr/sub | solution.py:45
  391.4 3.2 fusion.39
  398.1 2.9 dynamic-slice_bitcast_fusion.3
  401.0 5.6 %pad_maximum_fusion.7 = (bf16[768,1536]{0,1:T(8,128)(2,1)}, bf16[768,1536]{0,1:T(8,128)(2,1)S(1)}) fusion(bf16[384,3072]{0,1:T(8,128)(2,1)S(1)} %get-tuple-element.352, bf16[384,3072]{0,1:T(8,128)(2,1)S(1)} %get-tuple-element.353), kind=kLoop, calls=%fused_computation.13.clone.1 | loop fusion | flops 9437184 | bytes 9437184 | tf_op jit(solution)/shard_map/while/body/eval_jaxpr/concatenate | solution.py:81
  408.6 1.0 constant_dynamic-slice_fusion.3
  409.8 5.5 %fusion.38 = (f32[12,128]{1,0:T(8,128)S(1)}, f32[12,128,768]{2,1,0:T(8,128)}) fusion(pred[768]{0:T(1024)(128)(4,1)S(1)} %broadcast_bitcast_fusion.2, bf16[128,12,128]{0,2,1:T(8,128)(2,1)S(1)} %bitcast.55, bf16[768,12,128]{0,2,1:T(8,128)(2,1)} %bitcast.52), kind=kOutput, calls=%fused_computation.50.clone.1 | convolution fusion | flops 306709248 | bytes 7478016 | tf_op jit(solution)/shard_map/while/body/eval_jaxpr/sub | solution.py:45
  415.4 3.2 fusion.39
  419.6 3.5 broadcast_select_fusion
  423.1 10.6 %scatter_fusion = bf16[12,128,1536]{2,1,0:T(8,128)(2,1)} fusion(bf16[12,128,1536]{2,1,0:T(8,128)(2,1)} %bitcast.54, s32[9]{0:T(128)S(1)} %get-tuple-element.296, bf16[9,128,1536]{2,1,0:T(8,128)(2,1)S(1)} %broadcast_select_fusion), kind=kCustom, calls=%fused_computation.2 | custom fusion | bytes 10616868 | tf_op jit(solution)/shard_map/scatter | solution.py:95
  (79 shorter events, 16.1 us)
Async XLA Ops:
  11.5 81.4 %slice-start = ((s8[4718592]{0:T(1024)(128)(4,1)}), s8[524288]{0:T(1024)(128)(4,1)S(1)}, s32[]{:S(2)}) async-start(s8[4718592]{0:T(1024)(128)(4,1)} %bitcast.49), calls=%async_computation | async-start | bytes 1048576
  18.2 74.7 %slice-start.1 = ((s8[4718592]{0:T(1024)(128)(4,1)}), s8[4194304]{0:T(1024)(128)(4,1)S(1)}, s32[]{:S(2)}) async-start(s8[4718592]{0:T(1024)(128)(4,1)} %bitcast.49), calls=%async_computation.1 | async-start | bytes 8388608
  18.2 74.7 %copy-start = (bf16[4,384,1536]{1,2,0:T(8,128)(2,1)S(1)}, bf16[4,384,1536]{1,2,0:T(8,128)(2,1)}, u32[]{:S(2)}) copy-start(bf16[4,384,1536]{1,2,0:T(8,128)(2,1)} %copy.19) | copy-start | bytes 14155780
  21.4 70.6 %collective-permute-start = (bf16[4,128,3072]{1,2,0:T(8,128)(2,1)S(1)}, bf16[4,128,3072]{1,2,0:T(8,128)(2,1)S(1)}, u32[]{:S(2)}, u32[]{:S(2)}) collective-permute-start(bf16[4,128,3072]{1,2,0:T(8,128)(2,1)S(1)} %get-tuple-element.293), channel_id=1, source_target_pairs={{0,1},{1,2},{2,3},{3,4},{4,5},{5,6},{6,7},{8,9},{9,10},{10,11},{11... | collective-permute-start | bytes 9437192 | tf_op jit(solution)/shard_map/ppermute | solution.py:20
  23.5 81.1 %copy-start.5 = (s32[4,3]{1,0:T(4,128)S(1)}, s32[4,3]{1,0:T(4,128)}, u32[]{:S(2)}) copy-start(s32[4,3]{1,0:T(4,128)} %param.13) | copy-start | bytes 148
  23.6 81.2 %copy-start.4 = (s32[4,3,6]{2,0,1:T(4,128)S(1)}, s32[4,3,6]{2,0,1:T(4,128)}, u32[]{:S(2)}) copy-start(s32[4,3,6]{2,0,1:T(4,128)} %param.12) | copy-start | bytes 868
  23.6 69.4 %collective-permute-start.1 = (bf16[4,128,3072]{1,2,0:T(8,128)(2,1)S(1)}, bf16[4,128,3072]{1,2,0:T(8,128)(2,1)S(1)}, u32[]{:S(2)}, u32[]{:S(2)}) collective-permute-start(bf16[4,128,3072]{1,2,0:T(8,128)(2,1)S(1)} %get-tuple-element.294), channel_id=1, source_target_pairs={{1,0},{2,1},{3,2},{4,3},{5,4},{6,5},{7,6},{9,8},{10,9},{11,10},{12... | collective-permute-start | bytes 9437192 | tf_op jit(solution)/shard_map/ppermute | solution.py:22
  92.0 9.0 %copy-start.1 = (bf16[4,128,3072]{1,2,0:T(8,128)(2,1)}, bf16[4,128,3072]{1,2,0:T(8,128)(2,1)S(1)}, u32[]{:S(2)}) copy-start(bf16[4,128,3072]{1,2,0:T(8,128)(2,1)S(1)} %collective-permute-done) | copy-start | bytes 9437188
  92.9 8.0 %copy-start.3 = (bf16[4,128,3072]{1,2,0:T(8,128)(2,1)}, bf16[4,128,3072]{1,2,0:T(8,128)(2,1)S(1)}, u32[]{:S(2)}) copy-start(bf16[4,128,3072]{1,2,0:T(8,128)(2,1)S(1)} %collective-permute-done.1) | copy-start | bytes 9437188
  101.0 85.5 %collective-permute-start.2 = (bf16[1,640,3072]{1,2,0:T(8,128)(2,1)}, bf16[1,640,3072]{1,2,0:T(8,128)(2,1)}, u32[]{:S(2)}, u32[]{:S(2)}) collective-permute-start(bf16[1,640,3072]{1,2,0:T(8,128)(2,1)} %pad_maximum_fusion.1), channel_id=1, source_target_pairs={{0,8},{8,16},{16,24},{1,9},{9,17},{17,25},{2,10},{10,18},{18,26},{... | collective-permute-start | bytes 11796488 | tf_op jit(solution)/shard_map/ppermute | solution.py:32
  104.6 81.8 %copy-start.2 = (bf16[4,128,3072]{1,2,0:T(8,128)(2,1)S(1)}, bf16[4,128,3072]{1,2,0:T(8,128)(2,1)}, u32[]{:S(2)}) copy-start(bf16[4,128,3072]{1,2,0:T(8,128)(2,1)} %copy-done.1) | copy-start | bytes 9437188
where the time goes:
time: 441 us; the launch traced here: 434 us
  waiting for transfers between devices  139 us (32%)
  local copies, waits for them, and re-layouts  86.4 us (20%)
  other arithmetic  83.8 us (19%)
  matrix products  78.8 us (18%)
  loops' own time  34.9 us (8%)
  starting transfers between devices  10.4 us (2%)
    ppermute x1, waiting for transfers between devices, from_behind(): return lax.ppermute(block, axis, route)  74.5 us
    ppermute x1, waiting for transfers between devices, extended_2(): lax.ppermute(tail, axis, [(i, (i + 1) % count) for i in range(ends)])  63.9 us
    concatenate x9, other arithmetic, attend_one(): gathered = jnp.concatenate(pieces, axis=0)  50.5 us
    sub x9, matrix products, attend_block(): exponentials = jnp.exp(scores - row_max)  49.8 us
    another operation x1, loops' own time, local(): attended = lax.map(attend_one, slots_used)  34.9 us
    dot_general x9, matrix products, attend_block(): jnp.einsum('hqk,khe->qhe', weights, values_h, preferred_element_type=jnp....  28.9 us
    squeeze x9, local copies, waits for them, and re-layouts, attend_one(): pieces.append(window[0])  25.8 us
    unnamed x20, local copies, waits for them, and re-layouts  18.2 us
  transfers between devices with their start and end apart: 3, of which 3 were waited for; matrix products, arithmetic and copies ran while one was open for 2% of the time, Pallas kernels for 0%

commit v1 on v0

v1 whole, which is shorter than its diff:
```python
import functools
import math

import jax
import jax.numpy as jnp
from jax import lax
from jax.experimental import pallas as pl
from jax.experimental.pallas import tpu as pltpu
from jax.sharding import PartitionSpec as P

HEAD_DIM = 128
BLK = 128
GROUP = 3


def shift(block, axis, distance):
    count = lax.axis_size(axis)
    pairs = [(i, i + distance) for i in range(count) if 0 <= i + distance < count]
    return lax.ppermute(block, axis, pairs)


def frame_body(frame, blocks, heads, allow_ref, flag_ref, q_ref, cached_ref, *refs):
    kc, vc, kp, vp, klc, vlc, krc, vrc, klp, vlp, krp, vrp = refs[:12]
    out_ref = refs[-1]
    current = (klc, kc, krc), (vlc, vc, vrc)
    previous = (klp, kp, krp), (vlp, vp, vrp)
    scale2 = math.log2(math.e) * HEAD_DIM ** (-0.5)
    ones = jnp.ones((BLK, HEAD_DIM), jnp.bfloat16)

    def piece(sides, column, cols):
        left, own, right = sides
        if column < 0:
            return left[..., cols].reshape(BLK, HEAD_DIM)
        if column >= blocks:
            return right[..., cols].reshape(BLK, HEAD_DIM)
        return own[..., column * BLK : (column + 1) * BLK, cols].reshape(BLK, HEAD_DIM)

    for b in range(blocks):
        rows = slice(b * BLK, (b + 1) * BLK)
        flagged = flag_ref[frame, b] > 0

        @pl.when(flagged)
        def _():
            allowed = [allow_ref[frame, b * 6 + n] > 0 for n in range(6)]
            for h in range(heads):
                cols = slice(h * HEAD_DIM, (h + 1) * HEAD_DIM)
                query = q_ref[0, rows, cols]
                scores = []
                top = None
                for n in range(6):
                    keys = piece((current, previous)[n // 3][0], b + n % 3 - 1, cols)
                    s = lax.dot_general(
                        query, keys, (((1,), (1,)), ((), ())), preferred_element_type=jnp.float32
                    )
                    scores.append(s)
                    t = s if n == 1 else s + jnp.where(allowed[n], 0.0, -jnp.inf)
                    top = t if top is None else jnp.maximum(top, t)
                row_top = jnp.max(top, axis=1, keepdims=True) * scale2
                weights = []
                values = []
                for n in range(6):
                    base = row_top if n == 1 else row_top + jnp.where(allowed[n], 0.0, jnp.inf)
                    weights.append(jnp.exp2(scores[n] * scale2 - base).astype(jnp.bfloat16))
                    part = piece((current, previous)[n // 3][1], b + n % 3 - 1, cols)
                    values.append(jnp.concatenate([part, ones], axis=1))
                total = jnp.dot(
                    jnp.concatenate(weights, axis=1),
                    jnp.concatenate(values, axis=0),
                    preferred_element_type=jnp.float32,
                )
                out_ref[0, rows, cols] = (total[:, :HEAD_DIM] / total[:, HEAD_DIM:]).astype(out_ref.dtype)

        @pl.when(jnp.logical_not(flagged))
        def _():
            out_ref[0, rows, :] = cached_ref[0, rows, :]


def attend_frame(frame, q, k, v, cached, allowed, flags, halos, behind, out):
    frames, tokens, width = q.shape
    blocks = tokens // BLK
    group = GROUP if (width // HEAD_DIM) % GROUP == 0 else 1
    gw = group * HEAD_DIM

    def whole(f):
        return pl.BlockSpec((1, tokens, gw), lambda g: (f, 0, g))

    def pair(kv, f, n):
        return pl.BlockSpec((1, 1, n, gw), lambda g: (kv, f, 0, g))

    smem = pl.BlockSpec(memory_space=pltpu.SMEM)
    args = [allowed, flags, q, cached, k, v]
    specs = [smem, smem, whole(frame), whole(frame), whole(frame), whole(frame)]
    if frame > 0:
        args += [k, v]
        specs += [whole(frame - 1), whole(frame - 1)]
        rims = [halos[frame], halos[frame - 1]]
    else:
        prev, prev_rims = behind
        args += [prev, prev]
        specs += [pair(0, 0, tokens), pair(1, 0, tokens)]
        rims = [halos[frame], prev_rims]
    for left, right, place in rims:
        args += [left, left, right, right]
        specs += [pair(0, place, BLK), pair(1, place, BLK)] * 2
    aliases = {}
    if out is not None:
        aliases = {len(args): 0}
        args.append(out)
        specs.append(pl.BlockSpec(memory_space=pl.ANY))
    work = 4 * tokens * 6 * BLK * width
    return pl.pallas_call(
        functools.partial(frame_body, frame, blocks, group),
        grid=(width // gw,),
        in_specs=specs,
        out_specs=whole(frame),
        out_shape=jax.ShapeDtypeStruct(q.shape, q.dtype),
        input_output_aliases=aliases,
        compiler_params=pltpu.CompilerParams(vmem_limit_bytes=40 << 20),
        cost_estimate=pl.CostEstimate(
            flops=4 * work, bytes_accessed=12 * tokens * width * 2, transcendentals=0
        ),
        name=f"attend_frame_{frame}",
    )(*args)


def local(q, k, v, cached, pattern, refresh):
    frames, tokens, width = q.shape
    blocks = tokens // BLK
    last = frames - 1

    frame_at = lax.axis_index("frame") * frames + jnp.arange(frames, dtype=jnp.int32)
    block_at = lax.axis_index("tile") * blocks + jnp.arange(blocks, dtype=jnp.int32)
    n = jnp.arange(6, dtype=jnp.int32)
    spatial = block_at[None, :, None] + (n % 3 - 1)[None, None, :]
    inside = (
        (frame_at[:, None, None] - (n // 3)[None, None, :] >= 0)
        & (spatial >= 0)
        & (spatial < blocks * lax.axis_size("tile"))
    )
    allowed = jnp.where(inside, pattern, 0).reshape(frames, blocks * 6)

    prev = shift(jnp.stack([k[last:], v[last:]]), "frame", 1)
    halos = [None] * frames
    half = max(frames // 2, 1)
    starts = list(range(0, frames, half))[::-1]
    for start in starts:
        stop = min(start + half, frames)
        tail = jnp.stack([k[start:stop, tokens - BLK :], v[start:stop, tokens - BLK :]])
        head = jnp.stack([k[start:stop, :BLK], v[start:stop, :BLK]])
        left = shift(tail, "tile", 1)
        right = shift(head, "tile", -1)
        for f in range(start, stop):
            halos[f] = (left, right, f - start)
    prev_left = shift(prev[:, :, tokens - BLK :], "tile", 1)
    prev_right = shift(prev[:, :, :BLK], "tile", -1)
    behind = (prev, (prev_left, prev_right, 0))

    out = None
    for frame in range(frames - 1, -1, -1):
        out = attend_frame(frame, q, k, v, cached, allowed, refresh, halos, behind, out)
    return out


def solution(mesh):
    wide = P("frame", "tile", None)
    return jax.shard_map(
        local,
        mesh=mesh,
        in_specs=(wide, wide, wide, wide, wide, P("frame", "tile")),
        out_specs=wide,
        check_vma=False,
    )
```

time: 441 us -> 133 us (0.30); the launches traced: 434 us -> 134 us
  waiting for transfers between devices: 139 us -> 31.7 us
  matrix products: 78.8 us -> 0 us
  other arithmetic: 83.8 us -> 7.02 us
  local copies, waits for them, and re-layouts: 86.4 us -> 11.4 us
  Pallas kernels: 0 us -> 60.6 us
  loops' own time: 34.9 us -> 0 us
  starting transfers between devices: 10.4 us -> 23.1 us
    ppermute x3 -> x7, waiting for transfers between devices: 139 us -> 31.7 us  [shift(): return lax.ppermute(block, axis, pairs)]
    concatenate x11 -> x0, other arithmetic: 75.6 us -> none  [the longest x9 50.5 us: attend_one(): gathered = jnp.concatenate(pieces, axis=0)]
    pallas_call x0 -> x4, Pallas kernels: none -> 60.6 us  [attend_frame(): pl.pallas_call(functools.partial(frame_body, frame, blocks, group), grid=...]
    sub x9 -> x0, matrix products: 49.8 us -> none  [attend_block(): exponentials = jnp.exp(scores - row_max)]
    another operation x1 -> x0, loops' own time: 34.9 us -> none  [local(): attended = lax.map(attend_one, slots_used)]
    dot_general x9 -> x0, matrix products: 28.9 us -> none  [attend_block(): jnp.einsum('hqk,khe->qhe', weights, values_h, preferred_element_type=jnp....]
    squeeze x9 -> x0, local copies, waits for them, and re-layouts: 25.8 us -> none  [attend_one(): pieces.append(window[0])]
    dynamic_slice x27 -> x0, local copies, waits for them, and re-layouts: 16.6 us -> none  [the longest x18 11.2 us: attend_one(): query_blocks[position]]
  transfers between devices with their start and end apart: 3 -> 7, of which waited for: 3 -> 3; matrix products, arithmetic and copies ran while one was open for 2% -> 7% of each run, Pallas kernels for 0% -> 31%
where the time goes in v1:
time: 133 us; the launch traced here: 134 us
  Pallas kernels  60.6 us (46%)
  waiting for transfers between devices  31.7 us (24%)
  starting transfers between devices  23.1 us (17%)
  local copies, waits for them, and re-layouts  11.4 us (9%)
  other arithmetic  7.02 us (5%)
    pallas_call x4, Pallas kernels, attend_frame(): pl.pallas_call(functools.partial(frame_body, frame, blocks, group), grid=...  60.6 us
    ppermute x7, waiting for transfers between devices, shift(): return lax.ppermute(block, axis, pairs)  31.7 us
    ppermute x7, starting transfers between devices, shift(): return lax.ppermute(block, axis, pairs)  23.1 us
    unnamed x12, local copies, waits for them, and re-layouts  4.7 us
    another operation x1, local copies, waits for them, and re-layouts, local(): head = jnp.stack([k[start:stop, :BLK], v[start:stop, :BLK]])  3.21 us
  transfers between devices with their start and end apart: 7, of which 3 were waited for; matrix products, arithmetic and copies ran while one was open for 7% of the time, Pallas kernels for 31%

profile of v1, /device:TPU:20, one launch (start us, length us, event | category | flops | bytes accessed | tf_op | source)
XLA Modules:
  0.0 134.1 jit_solution(5290212254303372375)
XLA Ops:
  0.0 3.2 %slice_bitcast_fusion.2 = (bf16[1,2,128,1536]{3,2,1,0:T(8,128)(2,1)S(1)}, bf16[1,2,128,1536]{3,2,1,0:T(8,128)(2,1)S(1)}, bf16[1,2,128,1536]{3,2,1,0:T(8,128)(2,1...) fusion(bf16[4,384,1536]{2,1,0:T(8,128)(2,1)} %refs_1_.7, ...), kind=kLoop, calls=%fused_computation.7 | loop fusion | bytes 12582912 | tf_op jit(solution)/shard_map/stack | solution.py:149
  3.2 1.3 pad_maximum_fusion.3
  4.5 1.9 %collective-permute-start.5 = (bf16[2,2,128,1536]{3,2,1,0:T(8,128)(2,1)}, bf16[2,2,128,1536]{3,2,1,0:T(8,128)(2,1)}, u32[]{:S(2)}, u32[]{:S(2)}) collective-permute-start(bf16[2,2,128,1536]{3,2,1,0:T(8,128)(2,1)} %pad_maximum_fusion.3), channel_id=1, source_target_pairs={{0,1},{1,2},{2,3},{3,4},{4,5},{5,6},{6,7},{8,9},{9,10},{10,11},{11... | collective-permute-start | bytes 4718600 | tf_op jit(solution)/shard_map/ppermute | solution.py:19
  6.4 1.8 %slice_bitcast_fusion = (bf16[1,1,384,1536]{3,2,1,0:T(8,128)(2,1)S(1)}, bf16[1,1,384,1536]{3,2,1,0:T(8,128)(2,1)S(1)}) fusion(bf16[4,384,1536]{2,1,0:T(8,128)(2,1)} %refs_1_.7, bf16[4,384,1536]{2,1,0:T(8,128)(2,1)} %refs_0_.7), kind=kLoop, calls=%fused_computation.5 | loop fusion | bytes 4718592 | tf_op jit(solution)/shard_map/stack | solution.py:142
  8.2 1.6 %pad_maximum_fusion = bf16[2,1,384,1536]{3,2,1,0:T(8,128)(2,1)} fusion(bf16[1,1,384,1536]{3,2,1,0:T(8,128)(2,1)S(1)} %get-tuple-element.17, bf16[1,1,384,1536]{3,2,1,0:T(8,128)(2,1)S(1)} %get-tuple-element.18), kind=kLoop, calls=%fused_computation | loop fusion | flops 1179648 | bytes 4718592 | tf_op jit(solution)/shard_map/stack | solution.py:142
  9.8 3.5 %collective-permute-start = (bf16[2,1,384,1536]{3,2,1,0:T(8,128)(2,1)}, bf16[2,1,384,1536]{3,2,1,0:T(8,128)(2,1)}, u32[]{:S(2)}, u32[]{:S(2)}) collective-permute-start(bf16[2,1,384,1536]{3,2,1,0:T(8,128)(2,1)} %pad_maximum_fusion), channel_id=1, source_target_pairs={{0,8},{8,16},{16,24},{1,9},{9,17},{17,25},{2,10},{10,18},{18,26},{... | collective-permute-start | bytes 7077896 | tf_op jit(solution)/shard_map/ppermute | solution.py:19
  13.3 1.3 pad_maximum_fusion.4
  14.6 4.2 %collective-permute-start.6 = (bf16[2,2,128,1536]{3,2,1,0:T(8,128)(2,1)}, bf16[2,2,128,1536]{3,2,1,0:T(8,128)(2,1)}, u32[]{:S(2)}, u32[]{:S(2)}) collective-permute-start(bf16[2,2,128,1536]{3,2,1,0:T(8,128)(2,1)} %pad_maximum_fusion.4), channel_id=1, source_target_pairs={{1,0},{2,1},{3,2},{4,3},{5,4},{6,5},{7,6},{9,8},{10,9},{11,10},{12... | collective-permute-start | bytes 4718600 | tf_op jit(solution)/shard_map/ppermute | solution.py:19
  18.8 1.4 %pad_maximum_fusion.1 = bf16[2,2,128,1536]{3,2,1,0:T(8,128)(2,1)} fusion(bf16[1,2,128,1536]{3,2,1,0:T(8,128)(2,1)S(1)} %get-tuple-element.12, bf16[1,2,128,1536]{3,2,1,0:T(8,128)(2,1)S(1)} %get-tuple-element.19), kind=kLoop, calls=%fused_computation.1 | loop fusion | flops 786432 | bytes 3145728 | tf_op jit(solution)/shard_map/stack | solution.py:148
  20.2 1.9 %collective-permute-start.1 = (bf16[2,2,128,1536]{3,2,1,0:T(8,128)(2,1)}, bf16[2,2,128,1536]{3,2,1,0:T(8,128)(2,1)S(1)}, u32[]{:S(2)}, u32[]{:S(2)}) collective-permute-start(bf16[2,2,128,1536]{3,2,1,0:T(8,128)(2,1)} %pad_maximum_fusion.1), channel_id=1, source_target_pairs={{0,1},{1,2},{2,3},{3,4},{4,5},{5,6},{6,7},{8,9},{9,10},{10,11},{11... | collective-permute-start | bytes 4718600 | tf_op jit(solution)/shard_map/ppermute | solution.py:19
  22.1 0.0 copy-start.3
  22.1 0.0 copy-start.2
  22.1 1.3 pad_maximum_fusion.2
  23.4 4.5 %collective-permute-start.2 = (bf16[2,2,128,1536]{3,2,1,0:T(8,128)(2,1)}, bf16[2,2,128,1536]{3,2,1,0:T(8,128)(2,1)S(1)}, u32[]{:S(2)}, u32[]{:S(2)}) collective-permute-start(bf16[2,2,128,1536]{3,2,1,0:T(8,128)(2,1)} %pad_maximum_fusion.2), channel_id=1, source_target_pairs={{1,0},{2,1},{3,2},{4,3},{5,4},{6,5},{7,6},{9,8},{10,9},{11,10},{12... | collective-permute-start | bytes 4718600 | tf_op jit(solution)/shard_map/ppermute | solution.py:19
  28.0 0.1 add_compare_fusion.1
  28.1 0.1 subtract_compare_fusion
  28.2 0.0 copy-done.3
  28.2 0.1 reshape.125.allow_ref
  28.3 5.3 %collective-permute-done.5.refs_4_.refs_5_.refs_8_.refs_9_ = bf16[2,2,128,1536]{3,2,1,0:T(8,128)(2,1)} collective-permute-done((bf16[2,2,128,1536]{3,2,1,0:T(8,128)(2,1)}, bf16[2,2,128,1536]{3,2,1,0:T(8,128)(2,1)}, u32[]{:S(2)}, u32[]{:S(2)}) %collective-permute-start.5) | collective-permute-done | bytes 1572896 | tf_op jit(solution)/shard_map/ppermute | solution.py:19
  33.6 20.4 %collective-permute-done.6.refs_6_.refs_7_.refs_10_.refs_11_ = bf16[2,2,128,1536]{3,2,1,0:T(8,128)(2,1)} collective-permute-done((bf16[2,2,128,1536]{3,2,1,0:T(8,128)(2,1)}, bf16[2,2,128,1536]{3,2,1,0:T(8,128)(2,1)}, u32[]{:S(2)}, u32[]{:S(2)}) %collective-permute-start.6) | collective-permute-done | bytes 1572896 | tf_op jit(solution)/shard_map/ppermute | solution.py:19
  54.0 0.0 copy-done.2
  54.0 0.0 copy-start
  54.0 2.3 %copy-done = bf16[4,384,1536]{2,1,0:T(8,128)(2,1)S(1)} copy-done((bf16[4,384,1536]{2,1,0:T(8,128)(2,1)S(1)}, bf16[4,384,1536]{2,1,0:T(8,128)(2,1)}, u32[]{:S(2)}) %copy-start) | copy-done | bytes 4718616
  56.3 0.0 copy-start.1
  56.3 2.3 %copy-done.1 = bf16[4,384,1536]{2,1,0:T(8,128)(2,1)S(1)} copy-done((bf16[4,384,1536]{2,1,0:T(8,128)(2,1)S(1)}, bf16[4,384,1536]{2,1,0:T(8,128)(2,1)}, u32[]{:S(2)}) %copy-start.1) | copy-done | bytes 4718616
  58.7 8.4 %attend_frame_3.1.refs_12_ = bf16[4,384,1536]{2,1,0:T(8,128)(2,1)} custom-call(s32[4,18]{1,0:T(4,128)S(1)} %reshape.125.allow_ref, s32[4,3]{1,0:T(4,128)S(1)} %copy-done.2, bf16[4,384,1536]{2,1,0:T(8,128)(2,1)S(1)} %copy-done, bf16[4,384,1536]{2,1,0:T(8,128)(2,1)S(1)} %copy-done.1, bf16[4,384,1536]{2,1,0:T(8,128)(2,1)} %refs_0_.7, ...), custom_call_target="tpu_custom_call" | custom-call | flops 7247757312 | bytes 14155776 | tf_op jit(solution)/shard_map/attend_frame_3/pallas_call | solution.py:111
  67.0 0.0 collective-permute-done.refs_2_.refs_3_
  67.0 0.0 slice-start
  67.0 1.6 %fusion.1 = (bf16[2,1,128,1536]{3,2,1,0:T(8,128)(2,1)S(1)}, bf16[2,1,128,1536]{3,2,1,0:T(8,128)(2,1)S(1)}) fusion(bf16[2,1,384,1536]{3,2,1,0:T(8,128)(2,1)} %collective-permute-done.refs_2_.refs_3_), kind=kLoop, calls=%fused_computation.27 | loop fusion | bytes 3145728 | tf_op jit(solution)/shard_map/slice | solution.py:155
  68.7 2.1 %collective-permute-start.3 = (bf16[2,1,128,1536]{3,2,1,0:T(8,128)(2,1)S(1)}, bf16[2,1,128,1536]{3,2,1,0:T(8,128)(2,1)S(1)}, u32[]{:S(2)}, u32[]{:S(2)}) collective-permute-start(bf16[2,1,128,1536]{3,2,1,0:T(8,128)(2,1)S(1)} %get-tuple-element.14), channel_id=1, source_target_pairs={{0,1},{1,2},{2,3},{3,4},{4,5},{5,6},{6,7},{8,9},{9,10},{10,11},{11... | collective-permute-start | bytes 2359304 | tf_op jit(solution)/shard_map/ppermute | solution.py:19
  70.7 0.0 slice-start.1
  70.8 5.0 %collective-permute-start.4 = (bf16[2,1,128,1536]{3,2,1,0:T(8,128)(2,1)S(1)}, bf16[2,1,128,1536]{3,2,1,0:T(8,128)(2,1)S(1)}, u32[]{:S(2)}, u32[]{:S(2)}) collective-permute-start(bf16[2,1,128,1536]{3,2,1,0:T(8,128)(2,1)S(1)} %get-tuple-element.13), channel_id=1, source_target_pairs={{1,0},{2,1},{3,2},{4,3},{5,4},{6,5},{7,6},{9,8},{10,9},{11,10},{12... | collective-permute-start | bytes 2359304 | tf_op jit(solution)/shard_map/ppermute | solution.py:19
  75.8 0.0 collective-permute-done.1.refs_8_.refs_9_.refs_4_.refs_5_
  75.8 6.0 %collective-permute-done.2.refs_10_.refs_11_.refs_6_.refs_7_ = bf16[2,2,128,1536]{3,2,1,0:T(8,128)(2,1)S(1)} collective-permute-done((bf16[2,2,128,1536]{3,2,1,0:T(8,128)(2,1)}, bf16[2,2,128,1536]{3,2,1,0:T(8,128)(2,1)S(1)}, u32[]{:S(2)}, u32[]{:S(2)}) %collective-permute-start.2) | collective-permute-done | bytes 1572896 | tf_op jit(solution)/shard_map/ppermute | solution.py:19
  81.8 19.3 %attend_frame_2.1.refs_12_ = bf16[4,384,1536]{2,1,0:T(8,128)(2,1)} custom-call(s32[4,18]{1,0:T(4,128)S(1)} %reshape.125.allow_ref, s32[4,3]{1,0:T(4,128)S(1)} %copy-done.2, bf16[4,384,1536]{2,1,0:T(8,128)(2,1)S(1)} %copy-done, bf16[4,384,1536]{2,1,0:T(8,128)(2,1)} %cached_ref.7, bf16[4,384,1536]{2,1,0:T(8,128)(2,1)} %refs_0_.7, ...), custom_call_target="tpu_custom_call", output_to_operand_aliasing={{}: (16, {})} | custom-call | flops 7247757312 | bytes 14155776 | tf_op jit(solution)/shard_map/attend_frame_2/pallas_call | solution.py:111
  101.1 0.0 slice-done
  101.1 0.0 slice-done.1
  101.1 13.8 %attend_frame_1.1.refs_12_ = bf16[4,384,1536]{2,1,0:T(8,128)(2,1)} custom-call(s32[4,18]{1,0:T(4,128)S(1)} %reshape.125.allow_ref, s32[4,3]{1,0:T(4,128)S(1)} %copy-done.2, bf16[4,384,1536]{2,1,0:T(8,128)(2,1)S(1)} %copy-done, bf16[4,384,1536]{2,1,0:T(8,128)(2,1)S(1)} %bitcast.21, bf16[4,384,1536]{2,1,0:T(8,128)(2,1)} %refs_0_.7, ...), custom_call_target="tpu_custom_call", output_to_operand_aliasing={{}: (16, {})} | custom-call | flops 7247757312 | bytes 14155776 | tf_op jit(solution)/shard_map/attend_frame_1/pallas_call | solution.py:111
  114.9 0.0 collective-permute-done.3.refs_8_.refs_9_
  114.9 0.0 collective-permute-done.4.refs_10_.refs_11_
  114.9 19.2 %attend_frame_0.1 = bf16[4,384,1536]{2,1,0:T(8,128)(2,1)} custom-call(s32[4,18]{1,0:T(4,128)S(1)} %reshape.125.allow_ref, s32[4,3]{1,0:T(4,128)S(1)} %copy-done.2, bf16[4,384,1536]{2,1,0:T(8,128)(2,1)S(1)} %copy-done, bf16[4,384,1536]{2,1,0:T(8,128)(2,1)} %cached_ref.7, bf16[4,384,1536]{2,1,0:T(8,128)(2,1)} %refs_0_.7, ...), custom_call_target="tpu_custom_call", output_to_operand_aliasing={{}: (16, {})} | custom-call | flops 7247757312 | bytes 14155776 | tf_op jit(solution)/shard_map/attend_frame_0/pallas_call | solution.py:111
  (7 shorter events, 0.0 us)
Async XLA Ops:
  4.5 29.1 %collective-permute-start.5 = (bf16[2,2,128,1536]{3,2,1,0:T(8,128)(2,1)}, bf16[2,2,128,1536]{3,2,1,0:T(8,128)(2,1)}, u32[]{:S(2)}, u32[]{:S(2)}) collective-permute-start(bf16[2,2,128,1536]{3,2,1,0:T(8,128)(2,1)} %pad_maximum_fusion.3), channel_id=1, source_target_pairs={{0,1},{1,2},{2,3},{3,4},{4,5},{5,6},{6,7},{8,9},{9,10},{10,11},{11... | collective-permute-start | bytes 4718600 | tf_op jit(solution)/shard_map/ppermute | solution.py:19
  9.8 57.2 %collective-permute-start = (bf16[2,1,384,1536]{3,2,1,0:T(8,128)(2,1)}, bf16[2,1,384,1536]{3,2,1,0:T(8,128)(2,1)}, u32[]{:S(2)}, u32[]{:S(2)}) collective-permute-start(bf16[2,1,384,1536]{3,2,1,0:T(8,128)(2,1)} %pad_maximum_fusion), channel_id=1, source_target_pairs={{0,8},{8,16},{16,24},{1,9},{9,17},{17,25},{2,10},{10,18},{18,26},{... | collective-permute-start | bytes 7077896 | tf_op jit(solution)/shard_map/ppermute | solution.py:19
  14.6 39.4 %collective-permute-start.6 = (bf16[2,2,128,1536]{3,2,1,0:T(8,128)(2,1)}, bf16[2,2,128,1536]{3,2,1,0:T(8,128)(2,1)}, u32[]{:S(2)}, u32[]{:S(2)}) collective-permute-start(bf16[2,2,128,1536]{3,2,1,0:T(8,128)(2,1)} %pad_maximum_fusion.4), channel_id=1, source_target_pairs={{1,0},{2,1},{3,2},{4,3},{5,4},{6,5},{7,6},{9,8},{10,9},{11,10},{12... | collective-permute-start | bytes 4718600 | tf_op jit(solution)/shard_map/ppermute | solution.py:19
  20.2 55.6 %collective-permute-start.1 = (bf16[2,2,128,1536]{3,2,1,0:T(8,128)(2,1)}, bf16[2,2,128,1536]{3,2,1,0:T(8,128)(2,1)S(1)}, u32[]{:S(2)}, u32[]{:S(2)}) collective-permute-start(bf16[2,2,128,1536]{3,2,1,0:T(8,128)(2,1)} %pad_maximum_fusion.1), channel_id=1, source_target_pairs={{0,1},{1,2},{2,3},{3,4},{4,5},{5,6},{6,7},{8,9},{9,10},{10,11},{11... | collective-permute-start | bytes 4718600 | tf_op jit(solution)/shard_map/ppermute | solution.py:19
  22.1 6.1 %copy-start.3 = (s32[4,3,6]{2,0,1:T(4,128)S(1)}, s32[4,3,6]{2,0,1:T(4,128)}, u32[]{:S(2)}) copy-start(s32[4,3,6]{2,0,1:T(4,128)} %param.10) | copy-start | bytes 868
  22.1 31.9 %copy-start.2 = (s32[4,3]{1,0:T(4,128)S(1)}, s32[4,3]{1,0:T(4,128)}, u32[]{:S(2)}) copy-start(s32[4,3]{1,0:T(4,128)} %flag_ref.7) | copy-start | bytes 148
  23.4 58.4 %collective-permute-start.2 = (bf16[2,2,128,1536]{3,2,1,0:T(8,128)(2,1)}, bf16[2,2,128,1536]{3,2,1,0:T(8,128)(2,1)S(1)}, u32[]{:S(2)}, u32[]{:S(2)}) collective-permute-start(bf16[2,2,128,1536]{3,2,1,0:T(8,128)(2,1)} %pad_maximum_fusion.2), channel_id=1, source_target_pairs={{1,0},{2,1},{3,2},{4,3},{5,4},{6,5},{7,6},{9,8},{10,9},{11,10},{12... | collective-permute-start | bytes 4718600 | tf_op jit(solution)/shard_map/ppermute | solution.py:19
  54.0 2.3 %copy-start = (bf16[4,384,1536]{2,1,0:T(8,128)(2,1)S(1)}, bf16[4,384,1536]{2,1,0:T(8,128)(2,1)}, u32[]{:S(2)}) copy-start(bf16[4,384,1536]{2,1,0:T(8,128)(2,1)} %q_ref.7) | copy-start | bytes 14155780
  56.3 2.3 %copy-start.1 = (bf16[4,384,1536]{2,1,0:T(8,128)(2,1)S(1)}, bf16[4,384,1536]{2,1,0:T(8,128)(2,1)}, u32[]{:S(2)}) copy-start(bf16[4,384,1536]{2,1,0:T(8,128)(2,1)} %cached_ref.7) | copy-start | bytes 14155780
  67.0 34.0 %slice-start = ((s8[4718592]{0:T(1024)(128)(4,1)}), s8[4194304]{0:T(1024)(128)(4,1)S(1)}, s32[]{:S(2)}) async-start(s8[4718592]{0:T(1024)(128)(4,1)} %bitcast.20), calls=%async_computation | async-start | bytes 8388608
  68.7 46.2 %collective-permute-start.3 = (bf16[2,1,128,1536]{3,2,1,0:T(8,128)(2,1)S(1)}, bf16[2,1,128,1536]{3,2,1,0:T(8,128)(2,1)S(1)}, u32[]{:S(2)}, u32[]{:S(2)}) collective-permute-start(bf16[2,1,128,1536]{3,2,1,0:T(8,128)(2,1)S(1)} %get-tuple-element.14), channel_id=1, source_target_pairs={{0,1},{1,2},{2,3},{3,4},{4,5},{5,6},{6,7},{8,9},{9,10},{10,11},{11... | collective-permute-start | bytes 2359304 | tf_op jit(solution)/shard_map/ppermute | solution.py:19
  70.7 30.3 %slice-start.1 = ((s8[4718592]{0:T(1024)(128)(4,1)}), s8[524288]{0:T(1024)(128)(4,1)S(1)}, s32[]{:S(2)}) async-start(s8[4718592]{0:T(1024)(128)(4,1)} %bitcast.20), calls=%async_computation.1 | async-start | bytes 1048576
  70.8 44.1 %collective-permute-start.4 = (bf16[2,1,128,1536]{3,2,1,0:T(8,128)(2,1)S(1)}, bf16[2,1,128,1536]{3,2,1,0:T(8,128)(2,1)S(1)}, u32[]{:S(2)}, u32[]{:S(2)}) collective-permute-start(bf16[2,1,128,1536]{3,2,1,0:T(8,128)(2,1)S(1)} %get-tuple-element.13), channel_id=1, source_target_pairs={{1,0},{2,1},{3,2},{4,3},{5,4},{6,5},{7,6},{9,8},{10,9},{11,10},{12... | collective-permute-start | bytes 2359304 | tf_op jit(solution)/shard_map/ppermute | solution.py:19

commit v2 on v1

--- a/solution.py
+++ b/solution.py
@@ -10,13 +10,30 @@
 
 HEAD_DIM = 128
 BLK = 128
-GROUP = 3
+GROUP = 6
+ROW = 4
 
 
-def shift(block, axis, distance):
+def shift(block, axis, distance, skip=lambda i, j: False):
     count = lax.axis_size(axis)
     pairs = [(i, i + distance) for i in range(count) if 0 <= i + distance < count]
-    return lax.ppermute(block, axis, pairs)
+    return lax.ppermute(block, axis, [p for p in pairs if not skip(*p)])
+
+
+def relayed_rims(tail, head):
+    count = lax.axis_size("tile")
+    if count % ROW or count == ROW:
+        return shift(tail, "tile", 1), shift(head, "tile", -1)
+    place = lax.axis_index("tile") % ROW
+    ups = range(ROW - 1, count - 1, ROW)
+    first = [(i, i + ROW) for i in ups] + [(i + 1, i + 1 - ROW) for i in ups]
+    second = [(i + ROW, i + 1) for i in ups] + [(i + 1 - ROW, i) for i in ups]
+    relay = lax.ppermute(jnp.where(place == 0, head, tail), "tile", first)
+    crosses = lambda i, j: i // ROW != j // ROW
+    left = shift(tail, "tile", 1, crosses)
+    right = shift(head, "tile", -1, crosses)
+    relay = lax.ppermute(relay, "tile", second)
+    return jnp.where(place == 0, relay, left), jnp.where(place == ROW - 1, relay, right)
 
 
 def frame_body(frame, blocks, heads, allow_ref, flag_ref, q_ref, cached_ref, *refs):
@@ -35,40 +52,44 @@
             return right[..., cols].reshape(BLK, HEAD_DIM)
         return own[..., column * BLK : (column + 1) * BLK, cols].reshape(BLK, HEAD_DIM)
 
+    def neighbours(part, column, cols):
+        pairs = [(current, previous)[n // 3][part] for n in range(6)]
+        return [piece(pairs[n], column + n % 3 - 1, cols) for n in range(6)]
+
     for b in range(blocks):
         rows = slice(b * BLK, (b + 1) * BLK)
         flagged = flag_ref[frame, b] > 0
 
         @pl.when(flagged)
         def _():
-            allowed = [allow_ref[frame, b * 6 + n] > 0 for n in range(6)]
-            for h in range(heads):
-                cols = slice(h * HEAD_DIM, (h + 1) * HEAD_DIM)
-                query = q_ref[0, rows, cols]
-                scores = []
-                top = None
-                for n in range(6):
-                    keys = piece((current, previous)[n // 3][0], b + n % 3 - 1, cols)
-                    s = lax.dot_general(
-                        query, keys, (((1,), (1,)), ((), ())), preferred_element_type=jnp.float32
-                    )
-                    scores.append(s)
-                    t = s if n == 1 else s + jnp.where(allowed[n], 0.0, -jnp.inf)
-                    top = t if top is None else jnp.maximum(top, t)
-                row_top = jnp.max(top, axis=1, keepdims=True) * scale2
-                weights = []
-                values = []
-                for n in range(6):
-                    base = row_top if n == 1 else row_top + jnp.where(allowed[n], 0.0, jnp.inf)
-                    weights.append(jnp.exp2(scores[n] * scale2 - base).astype(jnp.bfloat16))
-                    part = piece((current, previous)[n // 3][1], b + n % 3 - 1, cols)
-                    values.append(jnp.concatenate([part, ones], axis=1))
+            bias = [jnp.where(allow_ref[frame, b * 6 + n] > 0, 0.0, -jnp.inf) for n in range(6)]
+            columns = [slice(h * HEAD_DIM, (h + 1) * HEAD_DIM) for h in range(heads)]
+            scores = []
+            for cols in columns:
+                s = lax.dot_general(
+                    q_ref[0, rows, cols],
+                    jnp.concatenate(neighbours(0, b, cols), axis=0),
+                    (((1,), (1,)), ((), ())),
+                    preferred_element_type=jnp.float32,
+                )
+                parts = [s[:, n * BLK : (n + 1) * BLK] for n in range(6)]
+                scores.append([t if n == 1 else t + bias[n] for n, t in enumerate(parts)])
+            weights = []
+            for parts in scores:
+                top = jnp.max(functools.reduce(jnp.maximum, parts), axis=1, keepdims=True)
+                top = jnp.broadcast_to(top * scale2, (BLK, BLK))
+                weights.append([jnp.exp2(t * scale2 - top).astype(jnp.bfloat16) for t in parts])
+            results = []
+            for cols, parts in zip(columns, weights):
+                values = [jnp.concatenate([x, ones], axis=1) for x in neighbours(1, b, cols)]
                 total = jnp.dot(
-                    jnp.concatenate(weights, axis=1),
+                    jnp.concatenate(parts, axis=1),
                     jnp.concatenate(values, axis=0),
                     preferred_element_type=jnp.float32,
                 )
-                out_ref[0, rows, cols] = (total[:, :HEAD_DIM] / total[:, HEAD_DIM:]).astype(out_ref.dtype)
+                results.append((total[:, :HEAD_DIM] / total[:, HEAD_DIM:]).astype(out_ref.dtype))
+            for cols, result in zip(columns, results):
+                out_ref[0, rows, cols] = result
 
         @pl.when(jnp.logical_not(flagged))
         def _():
@@ -78,7 +99,7 @@
 def attend_frame(frame, q, k, v, cached, allowed, flags, halos, behind, out):
     frames, tokens, width = q.shape
     blocks = tokens // BLK
-    group = GROUP if (width // HEAD_DIM) % GROUP == 0 else 1
+    group = math.gcd(width // HEAD_DIM, GROUP)
     gw = group * HEAD_DIM
 
     def whole(f):
@@ -115,7 +136,7 @@
         out_specs=whole(frame),
         out_shape=jax.ShapeDtypeStruct(q.shape, q.dtype),
         input_output_aliases=aliases,
-        compiler_params=pltpu.CompilerParams(vmem_limit_bytes=40 << 20),
+        compiler_params=pltpu.CompilerParams(vmem_limit_bytes=60 << 20),
         cost_estimate=pl.CostEstimate(
             flops=4 * work, bytes_accessed=12 * tokens * width * 2, transcendentals=0
         ),
@@ -147,8 +168,10 @@
         stop = min(start + half, frames)
         tail = jnp.stack([k[start:stop, tokens - BLK :], v[start:stop, tokens - BLK :]])
         head = jnp.stack([k[start:stop, :BLK], v[start:stop, :BLK]])
-        left = shift(tail, "tile", 1)
-        right = shift(head, "tile", -1)
+        if start == 0:
+            left, right = relayed_rims(tail, head)
+        else:
+            left, right = shift(tail, "tile", 1), shift(head, "tile", -1)
         for f in range(start, stop):
             halos[f] = (left, right, f - start)
     prev_left = shift(prev[:, :, tokens - BLK :], "tile", 1)

time: 133 us -> 112 us (0.84)
  the two profiles are of different devices: /device:TPU:20 before, /device:TPU:1 now
where the time goes in v2:
time: 112 us; the launch traced here: 113 us
  Pallas kernels  32.2 us (29%)
  waiting for transfers between devices  29.9 us (27%)
  starting transfers between devices  29 us (26%)
  other arithmetic  11.2 us (10%)
  local copies, waits for them, and re-layouts  10.1 us (9%)
    pallas_call x4, Pallas kernels, attend_frame(): pl.pallas_call(functools.partial(frame_body, frame, blocks, group), grid=...  32.2 us
    ppermute x7, waiting for transfers between devices, shift(): return lax.ppermute(block, axis, [p for p in pairs if not skip(*p)])  29.9 us
    ppermute x7, starting transfers between devices, shift(): return lax.ppermute(block, axis, [p for p in pairs if not skip(*p)])  25.3 us
    select_n x1, other arithmetic, relayed_rims(): jnp.where(place == ROW - 1, relay, right)  4.33 us
    another operation x2, other arithmetic, local(): head = jnp.stack([k[start:stop, :BLK], v[start:stop, :BLK]])  3.72 us
    another operation x1, local copies, waits for them, and re-layouts, local(): head = jnp.stack([k[start:stop, :BLK], v[start:stop, :BLK]])  3.2 us
    unnamed x10, local copies, waits for them, and re-layouts  2.95 us
  transfers between devices with their start and end apart: 9, of which 2 were waited for; matrix products, arithmetic and copies ran while one was open for 11% of the time, Pallas kernels for 20%

profile of v2, /device:TPU:1, one launch (start us, length us, event | category | flops | bytes accessed | tf_op | source)
XLA Modules:
  0.0 112.7 jit_solution(364900811889290561)
XLA Ops:
  0.0 3.2 %slice_bitcast_fusion.2 = (bf16[1,2,128,1536]{3,2,1,0:T(8,128)(2,1)S(1)}, bf16[1,2,128,1536]{3,2,1,0:T(8,128)(2,1)S(1)}, bf16[1,2,128,1536]{3,2,1,0:T(8,128)(2,1...) fusion(bf16[4,384,1536]{2,1,0:T(8,128)(2,1)} %refs_1_.7, ...), kind=kLoop, calls=%fused_computation.10 | loop fusion | bytes 12582912 | tf_op jit(solution)/shard_map/stack | solution.py:170
  3.2 2.4 %pad_maximum_fusion.1 = (bf16[2,2,128,1536]{3,2,1,0:T(8,128)(2,1)}, bf16[2,2,128,1536]{3,2,1,0:T(8,128)(2,1)}, bf16[2,2,128,1536]{3,2,1,0:T(8,128)(2,1)}) fusion(bf16[1,2,128,1536]{3,2,1,0:T(8,128)(2,1)S(1)} %get-tuple-element.12, bf16[1,2,128,1536]{3,2,1,0:T(8,128)(2,1)S(1)} %get-tuple-element.24, bf16[1,2,128,1536]{3,2,1,0:T(8,128)(2,1)S(1)} %get-tuple-element.11, ...), kind=kLoop, calls=%fused_computation.1 | loop fusion | flops 2359296 | bytes 7864321 | tf_op jit(solution)/shard_map/stack | solution.py:170
  5.7 1.9 %collective-permute-start.1 = (bf16[2,2,128,1536]{3,2,1,0:T(8,128)(2,1)}, bf16[2,2,128,1536]{3,2,1,0:T(8,128)(2,1)}, u32[]{:S(2)}, u32[]{:S(2)}) collective-permute-start(bf16[2,2,128,1536]{3,2,1,0:T(8,128)(2,1)} %get-tuple-element.18), channel_id=1, source_target_pairs={{3,7},{4,0},{11,15},{12,8},{19,23},{20,16},{27,31},{28,24}} | collective-permute-start | bytes 4718600 | tf_op jit(solution)/shard_map/ppermute | solution.py:31
  7.6 1.3 %pad_maximum_fusion.3 = bf16[2,2,128,1536]{3,2,1,0:T(8,128)(2,1)} fusion(bf16[1,2,128,1536]{3,2,1,0:T(8,128)(2,1)S(1)} %get-tuple-element.10, bf16[1,2,128,1536]{3,2,1,0:T(8,128)(2,1)S(1)} %get-tuple-element.26), kind=kLoop, calls=%fused_computation.3 | loop fusion | flops 786432 | bytes 3145728 | tf_op jit(solution)/shard_map/stack | solution.py:169
  8.9 4.5 %collective-permute-start.7 = (bf16[2,2,128,1536]{3,2,1,0:T(8,128)(2,1)}, bf16[2,2,128,1536]{3,2,1,0:T(8,128)(2,1)S(1)}, u32[]{:S(2)}, u32[]{:S(2)}) collective-permute-start(bf16[2,2,128,1536]{3,2,1,0:T(8,128)(2,1)} %pad_maximum_fusion.3), channel_id=1, source_target_pairs={{0,1},{1,2},{2,3},{3,4},{4,5},{5,6},{6,7},{8,9},{9,10},{10,11},{11... | collective-permute-start | bytes 4718600 | tf_op jit(solution)/shard_map/ppermute | solution.py:20
  13.4 1.8 %slice_bitcast_fusion = (bf16[1,1,384,1536]{3,2,1,0:T(8,128)(2,1)S(1)}, bf16[1,1,384,1536]{3,2,1,0:T(8,128)(2,1)S(1)}) fusion(bf16[4,384,1536]{2,1,0:T(8,128)(2,1)} %refs_1_.7, bf16[4,384,1536]{2,1,0:T(8,128)(2,1)} %refs_0_.7), kind=kLoop, calls=%fused_computation.8 | loop fusion | bytes 4718592 | tf_op jit(solution)/shard_map/stack | solution.py:163
  15.2 1.6 %pad_maximum_fusion = bf16[2,1,384,1536]{3,2,1,0:T(8,128)(2,1)} fusion(bf16[1,1,384,1536]{3,2,1,0:T(8,128)(2,1)S(1)} %get-tuple-element.22, bf16[1,1,384,1536]{3,2,1,0:T(8,128)(2,1)S(1)} %get-tuple-element.23), kind=kLoop, calls=%fused_computation | loop fusion | flops 1179648 | bytes 4718592 | tf_op jit(solution)/shard_map/stack | solution.py:163
  16.8 4.6 %collective-permute-start = (bf16[2,1,384,1536]{3,2,1,0:T(8,128)(2,1)}, bf16[2,1,384,1536]{3,2,1,0:T(8,128)(2,1)}, u32[]{:S(2)}, u32[]{:S(2)}) collective-permute-start(bf16[2,1,384,1536]{3,2,1,0:T(8,128)(2,1)} %pad_maximum_fusion), channel_id=1, source_target_pairs={{0,8},{8,16},{16,24},{1,9},{9,17},{17,25},{2,10},{10,18},{18,26},{... | collective-permute-start | bytes 7077896 | tf_op jit(solution)/shard_map/ppermute | solution.py:20
  21.4 0.0 copy-start.4
  21.4 1.3 %pad_maximum_fusion.4 = bf16[2,2,128,1536]{3,2,1,0:T(8,128)(2,1)} fusion(bf16[1,2,128,1536]{3,2,1,0:T(8,128)(2,1)S(1)} %get-tuple-element.9, bf16[1,2,128,1536]{3,2,1,0:T(8,128)(2,1)S(1)} %get-tuple-element.27), kind=kLoop, calls=%fused_computation.4 | loop fusion | flops 786432 | bytes 3145728 | tf_op jit(solution)/shard_map/stack | solution.py:170
  22.7 1.9 %collective-permute-start.8 = (bf16[2,2,128,1536]{3,2,1,0:T(8,128)(2,1)}, bf16[2,2,128,1536]{3,2,1,0:T(8,128)(2,1)S(1)}, u32[]{:S(2)}, u32[]{:S(2)}) collective-permute-start(bf16[2,2,128,1536]{3,2,1,0:T(8,128)(2,1)} %pad_maximum_fusion.4), channel_id=1, source_target_pairs={{1,0},{2,1},{3,2},{4,3},{5,4},{6,5},{7,6},{9,8},{10,9},{11,10},{12... | collective-permute-start | bytes 4718600 | tf_op jit(solution)/shard_map/ppermute | solution.py:20
  24.6 4.5 %collective-permute-start.3 = (bf16[2,2,128,1536]{3,2,1,0:T(8,128)(2,1)}, bf16[2,2,128,1536]{3,2,1,0:T(8,128)(2,1)}, u32[]{:S(2)}, u32[]{:S(2)}) collective-permute-start(bf16[2,2,128,1536]{3,2,1,0:T(8,128)(2,1)} %get-tuple-element.19), channel_id=1, source_target_pairs={{0,1},{1,2},{2,3},{4,5},{5,6},{6,7},{8,9},{9,10},{10,11},{12,13},{... | collective-permute-start | bytes 4718600 | tf_op jit(solution)/shard_map/ppermute | solution.py:20
  29.2 0.1 add_compare_fusion.1
  29.3 0.0 collective-permute-done.1
  29.3 1.9 %collective-permute-start.4 = (bf16[2,2,128,1536]{3,2,1,0:T(8,128)(2,1)}, bf16[2,2,128,1536]{3,2,1,0:T(8,128)(2,1)}, u32[]{:S(2)}, u32[]{:S(2)}) collective-permute-start(bf16[2,2,128,1536]{3,2,1,0:T(8,128)(2,1)} %get-tuple-element.17), channel_id=1, source_target_pairs={{1,0},{2,1},{3,2},{5,4},{6,5},{7,6},{9,8},{10,9},{11,10},{13,12},{... | collective-permute-start | bytes 4718600 | tf_op jit(solution)/shard_map/ppermute | solution.py:20
  31.2 0.0 collective-permute-done.7.refs_4_.refs_5_.refs_8_.refs_9_
  31.2 0.0 copy-start
  31.2 1.8 %collective-permute-start.2 = (bf16[2,2,128,1536]{3,2,1,0:T(8,128)(2,1)}, bf16[2,2,128,1536]{3,2,1,0:T(8,128)(2,1)}, u32[]{:S(2)}, u32[]{:S(2)}) collective-permute-start(bf16[2,2,128,1536]{3,2,1,0:T(8,128)(2,1)} %collective-permute-done.1), channel_id=1, source_target_pairs={{7,4},{0,3},{15,12},{8,11},{23,20},{16,19},{31,28},{24,27}} | collective-permute-start | bytes 4718600 | tf_op jit(solution)/shard_map/ppermute | solution.py:35
  33.0 0.1 subtract_compare_fusion
  33.1 0.0 copy-done.4
  33.1 0.7 reshape.125.allow_ref
  33.8 16.4 %collective-permute-done.8.refs_6_.refs_7_.refs_10_.refs_11_ = bf16[2,2,128,1536]{3,2,1,0:T(8,128)(2,1)S(1)} collective-permute-done((bf16[2,2,128,1536]{3,2,1,0:T(8,128)(2,1)}, bf16[2,2,128,1536]{3,2,1,0:T(8,128)(2,1)S(1)}, u32[]{:S(2)}, u32[]{:S(2)}) %collective-permute-start.8) | collective-permute-done | bytes 1572896 | tf_op jit(solution)/shard_map/ppermute | solution.py:20
  50.2 0.0 copy-done
  50.2 0.0 copy-start.1
  50.2 1.1 %copy-done.1 = bf16[2,2,128,1536]{3,2,1,0:T(8,128)(2,1)} copy-done((bf16[2,2,128,1536]{3,2,1,0:T(8,128)(2,1)}, bf16[2,2,128,1536]{3,2,1,0:T(8,128)(2,1)S(1)}, u32[]{:S(2)}) %copy-start.1) | copy-done | bytes 1572888
  51.3 5.9 %attend_frame_3.1.refs_12_ = bf16[4,384,1536]{2,1,0:T(8,128)(2,1)} custom-call(s32[4,18]{1,0:T(4,128)} %reshape.125.allow_ref, s32[4,3]{1,0:T(4,128)} %flag_ref.7, bf16[4,384,1536]{2,1,0:T(8,128)(2,1)} %q_ref.7, bf16[4,384,1536]{2,1,0:T(8,128)(2,1)} %cached_ref.7, bf16[4,384,1536]{2,1,0:T(8,128)(2,1)} %refs_0_.7, bf16[4,384,1536]{2,1,0:T(8,128)(2,1)} %refs_1_.7, ...), custom_call_target="tpu_custom_call" | custom-call | flops 7247757312 | bytes 14155776 | tf_op jit(solution)/shard_map/attend_frame_3/pallas_call | solution.py:132
  57.2 13.5 %collective-permute-done.refs_2_.refs_3_ = bf16[2,1,384,1536]{3,2,1,0:T(8,128)(2,1)} collective-permute-done((bf16[2,1,384,1536]{3,2,1,0:T(8,128)(2,1)}, bf16[2,1,384,1536]{3,2,1,0:T(8,128)(2,1)}, u32[]{:S(2)}, u32[]{:S(2)}) %collective-permute-start) | collective-permute-done | bytes 2359328 | tf_op jit(solution)/shard_map/ppermute | solution.py:20
  70.7 1.5 %fusion.1 = (bf16[2,1,128,1536]{3,2,1,0:T(8,128)(2,1)S(1)}, bf16[2,1,128,1536]{3,2,1,0:T(8,128)(2,1)S(1)}) fusion(bf16[2,1,384,1536]{3,2,1,0:T(8,128)(2,1)} %collective-permute-done.refs_2_.refs_3_), kind=kLoop, calls=%fused_computation.30 | loop fusion | bytes 3145728 | tf_op jit(solution)/shard_map/slice | solution.py:178
  72.1 5.7 %collective-permute-start.5 = (bf16[2,1,128,1536]{3,2,1,0:T(8,128)(2,1)S(1)}, bf16[2,1,128,1536]{3,2,1,0:T(8,128)(2,1)S(1)}, u32[]{:S(2)}, u32[]{:S(2)}) collective-permute-start(bf16[2,1,128,1536]{3,2,1,0:T(8,128)(2,1)S(1)} %get-tuple-element.14), channel_id=1, source_target_pairs={{0,1},{1,2},{2,3},{3,4},{4,5},{5,6},{6,7},{8,9},{9,10},{10,11},{11... | collective-permute-start | bytes 2359304 | tf_op jit(solution)/shard_map/ppermute | solution.py:20
  77.9 2.1 %collective-permute-start.6 = (bf16[2,1,128,1536]{3,2,1,0:T(8,128)(2,1)S(1)}, bf16[2,1,128,1536]{3,2,1,0:T(8,128)(2,1)S(1)}, u32[]{:S(2)}, u32[]{:S(2)}) collective-permute-start(bf16[2,1,128,1536]{3,2,1,0:T(8,128)(2,1)S(1)} %get-tuple-element.13), channel_id=1, source_target_pairs={{1,0},{2,1},{3,2},{4,3},{5,4},{6,5},{7,6},{9,8},{10,9},{11,10},{12... | collective-permute-start | bytes 2359304 | tf_op jit(solution)/shard_map/ppermute | solution.py:20
  80.0 0.0 collective-permute-done.3
  80.0 0.0 collective-permute-done.4
  80.0 0.0 collective-permute-done.2
  80.0 4.3 %broadcast_select_fusion = (bf16[2,2,128,1536]{3,2,1,0:T(8,128)(2,1)}, bf16[2,2,128,1536]{3,2,1,0:T(8,128)(2,1)}) fusion(bf16[2,2,128,1536]{3,2,1,0:T(8,128)(2,1)} %collective-permute-done.2, bf16[2,2,128,1536]{3,2,1,0:T(8,128)(2,1)} %collective-permute-done.4, pred[]{:T(512)S(6)} %eq.12, bf16[2,2,128,1536]{3,2,1,0:T(8,128)(2,1)} %collective-permute-done.3, ...), kind=kLoop, calls=%fused_computation.5 | loop fusion | flops 1572864 | bytes 7864322 | tf_op jit(solution)/shard_map/jit(_where)/select_n | solution.py:36
  84.3 7.5 %attend_frame_2.1.refs_12_ = bf16[4,384,1536]{2,1,0:T(8,128)(2,1)} custom-call(s32[4,18]{1,0:T(4,128)} %reshape.125.allow_ref, s32[4,3]{1,0:T(4,128)} %flag_ref.7, bf16[4,384,1536]{2,1,0:T(8,128)(2,1)} %q_ref.7, bf16[4,384,1536]{2,1,0:T(8,128)(2,1)} %cached_ref.7, bf16[4,384,1536]{2,1,0:T(8,128)(2,1)} %refs_0_.7, ...), custom_call_target="tpu_custom_call", output_to_operand_aliasing={{}: (16, {})} | custom-call | flops 7247757312 | bytes 14155776 | tf_op jit(solution)/shard_map/attend_frame_2/pallas_call | solution.py:132
  91.8 9.5 %attend_frame_1.1.refs_12_ = bf16[4,384,1536]{2,1,0:T(8,128)(2,1)} custom-call(s32[4,18]{1,0:T(4,128)} %reshape.125.allow_ref, s32[4,3]{1,0:T(4,128)} %flag_ref.7, bf16[4,384,1536]{2,1,0:T(8,128)(2,1)} %q_ref.7, bf16[4,384,1536]{2,1,0:T(8,128)(2,1)} %cached_ref.7, bf16[4,384,1536]{2,1,0:T(8,128)(2,1)} %refs_0_.7, ...), custom_call_target="tpu_custom_call", output_to_operand_aliasing={{}: (16, {})} | custom-call | flops 7247757312 | bytes 14155776 | tf_op jit(solution)/shard_map/attend_frame_1/pallas_call | solution.py:132
  101.3 0.0 collective-permute-done.5.refs_8_.refs_9_
  101.3 0.0 copy-start.2
  101.3 0.0 collective-permute-done.6.refs_10_.refs_11_
  101.3 0.9 copy-done.2
  102.2 0.0 copy-start.3
  102.2 0.9 copy-done.3
  103.1 9.4 %attend_frame_0.1 = bf16[4,384,1536]{2,1,0:T(8,128)(2,1)} custom-call(s32[4,18]{1,0:T(4,128)} %reshape.125.allow_ref, s32[4,3]{1,0:T(4,128)} %flag_ref.7, bf16[4,384,1536]{2,1,0:T(8,128)(2,1)} %q_ref.7, bf16[4,384,1536]{2,1,0:T(8,128)(2,1)} %cached_ref.7, bf16[4,384,1536]{2,1,0:T(8,128)(2,1)} %refs_0_.7, ...), custom_call_target="tpu_custom_call", output_to_operand_aliasing={{}: (16, {})} | custom-call | flops 7247757312 | bytes 14155776 | tf_op jit(solution)/shard_map/attend_frame_0/pallas_call | solution.py:132
  (6 shorter events, 0.0 us)
Async XLA Ops:
  5.7 23.6 %collective-permute-start.1 = (bf16[2,2,128,1536]{3,2,1,0:T(8,128)(2,1)}, bf16[2,2,128,1536]{3,2,1,0:T(8,128)(2,1)}, u32[]{:S(2)}, u32[]{:S(2)}) collective-permute-start(bf16[2,2,128,1536]{3,2,1,0:T(8,128)(2,1)} %get-tuple-element.18), channel_id=1, source_target_pairs={{3,7},{4,0},{11,15},{12,8},{19,23},{20,16},{27,31},{28,24}} | collective-permute-start | bytes 4718600 | tf_op jit(solution)/shard_map/ppermute | solution.py:31
  8.9 22.3 %collective-permute-start.7 = (bf16[2,2,128,1536]{3,2,1,0:T(8,128)(2,1)}, bf16[2,2,128,1536]{3,2,1,0:T(8,128)(2,1)S(1)}, u32[]{:S(2)}, u32[]{:S(2)}) collective-permute-start(bf16[2,2,128,1536]{3,2,1,0:T(8,128)(2,1)} %pad_maximum_fusion.3), channel_id=1, source_target_pairs={{0,1},{1,2},{2,3},{3,4},{4,5},{5,6},{6,7},{8,9},{9,10},{10,11},{11... | collective-permute-start | bytes 4718600 | tf_op jit(solution)/shard_map/ppermute | solution.py:20
  16.8 53.9 %collective-permute-start = (bf16[2,1,384,1536]{3,2,1,0:T(8,128)(2,1)}, bf16[2,1,384,1536]{3,2,1,0:T(8,128)(2,1)}, u32[]{:S(2)}, u32[]{:S(2)}) collective-permute-start(bf16[2,1,384,1536]{3,2,1,0:T(8,128)(2,1)} %pad_maximum_fusion), channel_id=1, source_target_pairs={{0,8},{8,16},{16,24},{1,9},{9,17},{17,25},{2,10},{10,18},{18,26},{... | collective-permute-start | bytes 7077896 | tf_op jit(solution)/shard_map/ppermute | solution.py:20
  21.4 11.7 %copy-start.4 = (s32[4,3,6]{2,0,1:T(4,128)S(1)}, s32[4,3,6]{2,0,1:T(4,128)}, u32[]{:S(2)}) copy-start(s32[4,3,6]{2,0,1:T(4,128)} %param.10) | copy-start | bytes 868
  22.7 27.5 %collective-permute-start.8 = (bf16[2,2,128,1536]{3,2,1,0:T(8,128)(2,1)}, bf16[2,2,128,1536]{3,2,1,0:T(8,128)(2,1)S(1)}, u32[]{:S(2)}, u32[]{:S(2)}) collective-permute-start(bf16[2,2,128,1536]{3,2,1,0:T(8,128)(2,1)} %pad_maximum_fusion.4), channel_id=1, source_target_pairs={{1,0},{2,1},{3,2},{4,3},{5,4},{6,5},{7,6},{9,8},{10,9},{11,10},{12... | collective-permute-start | bytes 4718600 | tf_op jit(solution)/shard_map/ppermute | solution.py:20
  24.6 55.4 %collective-permute-start.3 = (bf16[2,2,128,1536]{3,2,1,0:T(8,128)(2,1)}, bf16[2,2,128,1536]{3,2,1,0:T(8,128)(2,1)}, u32[]{:S(2)}, u32[]{:S(2)}) collective-permute-start(bf16[2,2,128,1536]{3,2,1,0:T(8,128)(2,1)} %get-tuple-element.19), channel_id=1, source_target_pairs={{0,1},{1,2},{2,3},{4,5},{5,6},{6,7},{8,9},{9,10},{10,11},{12,13},{... | collective-permute-start | bytes 4718600 | tf_op jit(solution)/shard_map/ppermute | solution.py:20
  29.3 50.7 %collective-permute-start.4 = (bf16[2,2,128,1536]{3,2,1,0:T(8,128)(2,1)}, bf16[2,2,128,1536]{3,2,1,0:T(8,128)(2,1)}, u32[]{:S(2)}, u32[]{:S(2)}) collective-permute-start(bf16[2,2,128,1536]{3,2,1,0:T(8,128)(2,1)} %get-tuple-element.17), channel_id=1, source_target_pairs={{1,0},{2,1},{3,2},{5,4},{6,5},{7,6},{9,8},{10,9},{11,10},{13,12},{... | collective-permute-start | bytes 4718600 | tf_op jit(solution)/shard_map/ppermute | solution.py:20
  31.2 19.0 %copy-start = (bf16[2,2,128,1536]{3,2,1,0:T(8,128)(2,1)}, bf16[2,2,128,1536]{3,2,1,0:T(8,128)(2,1)S(1)}, u32[]{:S(2)}) copy-start(bf16[2,2,128,1536]{3,2,1,0:T(8,128)(2,1)S(1)} %collective-permute-done.7.refs_4_.refs_5_.refs_8_.refs_9_) | copy-start | bytes 4718596
  31.2 48.8 %collective-permute-start.2 = (bf16[2,2,128,1536]{3,2,1,0:T(8,128)(2,1)}, bf16[2,2,128,1536]{3,2,1,0:T(8,128)(2,1)}, u32[]{:S(2)}, u32[]{:S(2)}) collective-permute-start(bf16[2,2,128,1536]{3,2,1,0:T(8,128)(2,1)} %collective-permute-done.1), channel_id=1, source_target_pairs={{7,4},{0,3},{15,12},{8,11},{23,20},{16,19},{31,28},{24,27}} | collective-permute-start | bytes 4718600 | tf_op jit(solution)/shard_map/ppermute | solution.py:35
  50.2 1.1 %copy-start.1 = (bf16[2,2,128,1536]{3,2,1,0:T(8,128)(2,1)}, bf16[2,2,128,1536]{3,2,1,0:T(8,128)(2,1)S(1)}, u32[]{:S(2)}) copy-start(bf16[2,2,128,1536]{3,2,1,0:T(8,128)(2,1)S(1)} %collective-permute-done.8.refs_6_.refs_7_.refs_10_.refs_11_) | copy-start | bytes 4718596
  72.1 29.1 %collective-permute-start.5 = (bf16[2,1,128,1536]{3,2,1,0:T(8,128)(2,1)S(1)}, bf16[2,1,128,1536]{3,2,1,0:T(8,128)(2,1)S(1)}, u32[]{:S(2)}, u32[]{:S(2)}) collective-permute-start(bf16[2,1,128,1536]{3,2,1,0:T(8,128)(2,1)S(1)} %get-tuple-element.14), channel_id=1, source_target_pairs={{0,1},{1,2},{2,3},{3,4},{4,5},{5,6},{6,7},{8,9},{9,10},{10,11},{11... | collective-permute-start | bytes 2359304 | tf_op jit(solution)/shard_map/ppermute | solution.py:20
  77.9 23.4 %collective-permute-start.6 = (bf16[2,1,128,1536]{3,2,1,0:T(8,128)(2,1)S(1)}, bf16[2,1,128,1536]{3,2,1,0:T(8,128)(2,1)S(1)}, u32[]{:S(2)}, u32[]{:S(2)}) collective-permute-start(bf16[2,1,128,1536]{3,2,1,0:T(8,128)(2,1)S(1)} %get-tuple-element.13), channel_id=1, source_target_pairs={{1,0},{2,1},{3,2},{4,3},{5,4},{6,5},{7,6},{9,8},{10,9},{11,10},{12... | collective-permute-start | bytes 2359304 | tf_op jit(solution)/shard_map/ppermute | solution.py:20
  101.3 0.9 copy-start.2
  102.2 0.9 copy-start.3
